TPU v7x, 32 devices: a whole 2x2x4 slice. The times are simulated.
32 devices in a mesh: seq: 8 (over z, core), tp: 4 (over y, x).
Axes of the slice: x: 2, y: 2, z: 4, core: 2. Of those that a mesh axis runs over, the one named last changes fastest.
Arguments:
- hidden_in: bfloat16 [3072, 3584], P('seq'), may hold values from -48 to 48
- joined_inputs: bfloat16 [3072, 8192], P('seq', 'tp'), may hold values from -64 to 64
- lengths: int32 [4], replicated, may hold values from 1 to 1536, 3072 in all
- o_weight: bfloat16 [4096, 3584], P('tp'), may hold values from -0.09375 to 0.09375
- gate_up: float32 [2, 3584, 7168], P(None, ('seq', 'tp')), may hold values from -0.09375 to 0.09375
- down_weight: bfloat16 [7168, 3584], P('tp'), may hold values from -0.0625 to 0.0625
- next_weight: bfloat16 [3584, 8192], P(None, 'tp'), may hold values from -0.09375 to 0.09375
- post_attn_gain: float32 [3584], replicated, may hold values from 0.1 to 1.9
- pre_ffw_gain: float32 [3584], replicated, may hold values from 0.1 to 1.9
- post_ffw_gain: float32 [3584], replicated, may hold values from 0.1 to 1.9
- next_gain: float32 [3584], replicated, may hold values from 0.1 to 1.9
Outputs:
- next_qkv: bfloat16 [3072, 8192], P('seq', 'tp')
Inputs may be any that keep to these rules, and one draw needn't show every extreme that they name: The lengths of 4 prompts laid end to end; they sum to 3072 and the longest is exactly 1536.
All inputs are finite; a program needn't handle non-finite values.
Results may differ from a plain program's by a relative error of at most 0.022.
Values may be sent and summed in bfloat16 or wider, within the bound.
No kernel may reach another device: no remote copies, remote signals or barrier semaphores. Data moves between devices by JAX's collectives and lax.ppermute only.
A program may use at most 192 MiB of HBM per device.

v0:
```python
import jax
import jax.numpy as jnp
from jax import lax
from jax.sharding import PartitionSpec as P

HEADS = 16
KV_HEADS = 8
HEAD_DIM = 256


def rms_norm(values, gain):
    meansq = jnp.mean(values * values, axis=-1, keepdims=True)
    return values * lax.rsqrt(meansq + 1e-06) * gain


def local(
    hidden_in,
    joined_inputs,
    lengths,
    o_weight,
    gate_up,
    down_weight,
    next_weight,
    post_attn_gain,
    pre_ffw_gain,
    post_ffw_gain,
    next_gain,
):
    seq_count = lax.axis_size("seq")
    tp_count = lax.axis_size("tp")
    row_count = hidden_in.shape[0]
    model_width = hidden_in.shape[1]
    per_group = HEADS // KV_HEADS
    group_cols = (per_group + 2) * HEAD_DIM
    local_groups = joined_inputs.shape[1] // group_cols
    grouped = joined_inputs.reshape(row_count, local_groups, group_cols)
    queries = grouped[:, :, : per_group * HEAD_DIM].reshape(
        row_count, local_groups, per_group, HEAD_DIM
    )
    own_keys = grouped[:, :, per_group * HEAD_DIM : (per_group + 1) * HEAD_DIM]
    own_values = grouped[:, :, (per_group + 1) * HEAD_DIM :]
    keys_all, values_all = (
        lax.all_gather(own_keys, "seq", axis=0, tiled=True),
        lax.all_gather(own_values, "seq", axis=0, tiled=True),
    )
    total_rows = keys_all.shape[0]
    seq_index = lax.axis_index("seq")
    position = seq_index * row_count
    ends = jnp.cumsum(lengths)
    places = jnp.arange(total_rows, dtype=jnp.int32)
    prompt_ids = jnp.sum((places[:, None] >= ends[None, :]).astype(jnp.int32), axis=1)
    query_place = position + jnp.arange(row_count, dtype=jnp.int32)
    query_ids = lax.dynamic_slice_in_dim(prompt_ids, position, row_count, 0)
    scale = HEAD_DIM ** (-0.5)
    scores = (
        jnp.einsum("qgrd,kgd->qgrk", queries, keys_all, preferred_element_type=jnp.float32) * scale
    )
    allowed = (
        (query_ids[:, None] == prompt_ids[None, :]) & (places[None, :] <= query_place[:, None])
    )[:, None, None, :]
    scores = jnp.where(allowed, scores, -jnp.inf)
    peak = jnp.max(scores, axis=-1, keepdims=True)
    weights = jnp.where(allowed, jnp.exp(scores - peak), 0.0)
    norm_sum = jnp.sum(weights, axis=-1)
    blended = jnp.einsum(
        "qgrk,kgd->qgrd",
        weights.astype(jnp.bfloat16),
        values_all,
        preferred_element_type=jnp.float32,
    )
    blended = blended / norm_sum[..., None]
    attended = blended.astype(jnp.bfloat16).reshape(row_count, local_groups * per_group * HEAD_DIM)
    projected = jnp.dot(attended, o_weight, preferred_element_type=jnp.float32)

    def total_of(values):
        return lax.psum(values.astype(jnp.bfloat16), "tp").astype(jnp.float32)

    residual_mid = hidden_in.astype(jnp.float32) + rms_norm(total_of(projected), post_attn_gain)
    ffw_in = rms_norm(residual_mid, pre_ffw_gain).astype(jnp.bfloat16)
    server_low = gate_up.astype(jnp.bfloat16)
    stacked_rows = lax.all_gather(server_low, "seq", axis=1, tiled=True)
    local_units = lax.all_to_all(stacked_rows, "tp", split_axis=2, concat_axis=1, tiled=True)
    piece_rows = gate_up.shape[1]
    reordered = (
        ffw_in.reshape(row_count, seq_count, tp_count, piece_rows)
        .transpose(0, 2, 1, 3)
        .reshape(row_count, model_width)
    )
    gate = jnp.dot(reordered, local_units[0], preferred_element_type=jnp.float32)
    up_part = jnp.dot(reordered, local_units[1], preferred_element_type=jnp.float32)
    activated = (jax.nn.gelu(gate, approximate=True) * up_part).astype(jnp.bfloat16)
    ffw_out = jnp.dot(activated, down_weight, preferred_element_type=jnp.float32)
    residual_out = residual_mid + rms_norm(total_of(ffw_out), post_ffw_gain)
    next_in = rms_norm(residual_out, next_gain).astype(jnp.bfloat16)
    return jnp.dot(next_in, next_weight, preferred_element_type=jnp.float32).astype(jnp.bfloat16)


def solution(mesh):
    in_specs = (
        P("seq", None),
        P("seq", "tp"),
        P(),
        P("tp", None),
        P(None, ("seq", "tp"), None),
        P("tp", None),
        P(None, "tp"),
        P(),
        P(),
        P(),
        P(),
    )
    out_specs = P("seq", "tp")
    return jax.shard_map(local, mesh=mesh, in_specs=in_specs, out_specs=out_specs, check_vma=False)
```

profile of v0, /device:TPU:0, one launch (start us, length us, event | category | flops | bytes accessed | tf_op | source)
XLA Modules:
  0.0 898.3 jit_solution(8460055847567387025)
XLA Ops:
  6.5 9.4 %copy.57 = bf16[2,112,7168]{2,0,1:T(2,128)(2,1)} copy(f32[2,112,7168]{2,1,0:T(8,128)} %param.15) | data formatting | bytes 9633792 | tf_op args[4]
  16.0 227.0 %all-gather.8.cloned.1.call-done = bf16[2,896,7168]{2,0,1:T(2,128)(2,1)} async-done(((bf16[2,112,7168]{2,0,1:T(2,128)(2,1)}), bf16[2,896,7168]{2,0,1:T(2,128)(2,1)}) %all-gather.8.cloned.1.call-update) | async-done | bytes 25690128 | tf_op jit(solution)/shard_map/all_gather | solution.py:81
  243.0 84.6 %copy.47 = bf16[2,896,7168]{1,0,2:T(2,128)(2,1)} copy(bf16[2,896,7168]{2,0,1:T(2,128)(2,1)} %all-gather.8.cloned.1.call-done) | data formatting | bytes 51380224 | tf_op jit(solution)/shard_map/all_gather | solution.py:81
  327.6 8.7 all-to-all-start
  342.1 34.1 %all-gather.4.cloned.1.call-done = bf16[3072,2,256]{2,0,1:T(8,128)(2,1)} async-done(((bf16[384,2,256]{2,0,1:T(8,128)(2,1)}), bf16[3072,2,256]{2,0,1:T(8,128)(2,1)}) %all-gather.4.cloned.1.call-update) | async-done | bytes 3145744 | tf_op jit(solution)/shard_map/all_gather | solution.py:43
  376.2 11.3 %fusion.15 = f32[2,3072,384,2]{2,1,3,0:T(8,128)} fusion(bf16[384,2,2,256]{0,3,2,1:T(8,128)(2,1)S(1)} %bitcast.57, bf16[3072,2,256]{2,0,1:T(8,128)(2,1)} %all-gather.4.cloned.1.call-done), kind=kOutput, calls=%fused_computation.30 | convolution fusion | flops 2415919104 | bytes 22806528 | tf_op jit(solution)/shard_map/qgrd,kgd->qgrk/dot_general | solution.py:56
  387.4 20.2 %fusion.41 = (f32[384,2,2]{0,2,1:T(2,128)S(1)}, bf16[384,2,2,3072]{0,3,2,1:T(8,128)(2,1)}) fusion(f32[2,3072,384,2]{2,1,3,0:T(8,128)} %fusion.15, pred[384,3072]{0,1:T(8,128)(4,1)S(1)} %fusion.13), kind=kOutput, calls=%fused_computation.61 | output fusion | flops 37751808 | bytes 29497344 | tf_op jit(solution)/shard_map/sub | solution.py:63
  407.6 7.3 all-gather.6.cloned.1.call-done
  414.9 7.2 fusion.27
  422.2 7.7 convolution_convert_fusion.1
  429.9 12.8 %all-reduce.5.cloned.1.call-start = ((), (), s32[]{:S(2)}) async-start(), calls=%async_computation.5 | async-start | bytes 5505024 | tf_op jit(solution)/shard_map/psum | solution.py:76
  442.6 233.4 %all-reduce.3.cloned.1.call-done = bf16[384,3584]{1,0:T(8,128)(2,1)} async-done(((bf16[384,3584]{1,0:T(8,128)(2,1)}), bf16[384,3584]{1,0:T(8,128)(2,1)}) %all-reduce.3.cloned.1.call-update) | async-done | bytes 2752528 | tf_op jit(solution)/shard_map/psum | solution.py:76
  678.6 4.0 multiply_reduce_fusion.1
  682.6 5.1 multiply_convert_fusion.1
  687.7 4.5 copy.44
  695.8 15.5 %copy.48 = bf16[2,896,7168]{1,2,0:T(8,128)(2,1)S(1)} copy(bf16[2,896,7168]{1,0,2:T(2,128)(2,1)} %all-to-all-done) | data formatting | bytes 51380224 | tf_op jit(solution)/shard_map/all_to_all | solution.py:82
  711.3 8.9 fusion.39
  720.2 17.9 %copy.49 = bf16[1,4,896,1792]{3,2,1,0:T(8,128)(2,1)} copy(bf16[1,4,896,1792]{2,3,1,0:T(8,128)(2,1)} %get-tuple-element.5) | data formatting | bytes 25690112 | tf_op jit(solution)/shard_map/slice | solution.py:89
  738.1 17.9 %copy.50 = bf16[1,4,896,1792]{3,2,1,0:T(8,128)(2,1)} copy(bf16[1,4,896,1792]{2,3,1,0:T(8,128)(2,1)} %get-tuple-element.6) | data formatting | bytes 25690112 | tf_op jit(solution)/shard_map/slice | solution.py:90
  756.0 12.3 %fusion.42 = f32[384,1792]{1,0:T(8,128)} fusion(bf16[384,3584]{0,1:T(8,128)(2,1)} %bitcast.58, bf16[3584,1792]{1,0:T(8,128)(2,1)} %bitcast.52), kind=kOutput, calls=%fused_computation.62 | convolution fusion | flops 4932501504 | bytes 18350080 | tf_op jit(solution)/shard_map/dot_general | solution.py:89
  768.3 23.1 %convolution_convert_fusion = bf16[384,3584]{1,0:T(8,128)(2,1)} fusion(bf16[1792,3584]{1,0:T(8,128)(2,1)} %param.16, bf16[384,3584]{0,1:T(8,128)(2,1)} %bitcast.59, bf16[3584,1792]{1,0:T(8,128)(2,1)} %bitcast.53, f32[384,1792]{1,0:T(8,128)} %fusion.42), kind=kOutput, calls=%fused_computation.14 | convolution fusion | flops 9873260544 | bytes 33947648 | tf_op jit(solution)/shard_map/dot_general | solution.py:92
  791.4 80.8 %all-reduce.5.cloned.1.call-done = bf16[384,3584]{1,0:T(8,128)(2,1)} async-done(((bf16[384,3584]{1,0:T(8,128)(2,1)}), bf16[384,3584]{1,0:T(8,128)(2,1)}) %all-reduce.5.cloned.1.call-update) | async-done | bytes 2752528 | tf_op jit(solution)/shard_map/psum | solution.py:76
  874.8 4.8 multiply_reduce_fusion
  879.6 11.9 %convolution_convert_fusion.2 = bf16[384,2048]{1,0:T(8,128)(2,1)} fusion(bf16[3584,2048]{1,0:T(8,128)(2,1)} %param.17, f32[3584]{0:T(1024)S(1)} %copy-done.7, f32[384]{0:T(512)S(1)} %add_rsqrt_fusion, bf16[384,3584]{1,0:T(8,128)(2,1)S(1)} %copy-done.2, bf16[384,3584]{1,0:T(8,128)(2,1)S(1)} %copy-done, bf16[384,3584]{1,0:T(8,128)(2,1)S(1)} %copy-done.1, ...), kind=kOutput, calls=%fused_computation.33 | convolution fusion | flops 5654446080 | bytes 24558080 | tf_op jit(solution)/shard_map/dot_general | solution.py:95
  (44 shorter events, 14.5 us)
Async XLA Ops:
  6.5 236.5 %all-gather.8.cloned.1.call-start = ((), (), s32[]{:S(2)}) async-start(), calls=%async_computation.4 | async-start | bytes 28901376 | tf_op jit(solution)/shard_map/all_gather | solution.py:81
  327.6 8.8 copy-start.3
  327.6 368.2 %all-to-all-start = ((bf16[2,896,7168]{1,0,2:T(2,128)(2,1)}), bf16[2,896,7168]{1,0,2:T(2,128)(2,1)}, u32[]{:S(2)}, u32[]{:S(2)}) async-start(bf16[2,896,7168]{1,0,2:T(2,128)(2,1)} %copy.47), calls=%async_computation | async-start | bytes 51380224 | tf_op jit(solution)/shard_map/all_to_all | solution.py:82
  336.3 4.0 copy-start.8
  336.3 39.9 %all-gather.4.cloned.1.call-start = ((), (), s32[]{:S(2)}) async-start(), calls=%async_computation.1 | async-start | bytes 3538944 | tf_op jit(solution)/shard_map/all_gather | solution.py:43
  339.0 75.9 %all-gather.6.cloned.1.call-start = ((), (), s32[]{:S(2)}) async-start(), calls=%async_computation.2 | async-start | bytes 3538944 | tf_op jit(solution)/shard_map/all_gather | solution.py:44
  339.8 336.2 %all-reduce.3.cloned.1.call-start = ((), (), s32[]{:S(2)}) async-start(), calls=%async_computation.3 | async-start | bytes 5505024 | tf_op jit(solution)/shard_map/psum | solution.py:76
  429.8 248.7 %copy-start.4 = (f32[3584]{0:T(1024)S(1)}, f32[3584]{0:T(1024)}, u32[]{:S(2)}) copy-start(f32[3584]{0:T(1024)} %param.18) | copy-start | bytes 43012
  429.8 252.8 %copy-start.5 = (f32[3584]{0:T(1024)S(1)}, f32[3584]{0:T(1024)}, u32[]{:S(2)}) copy-start(f32[3584]{0:T(1024)} %param.19) | copy-start | bytes 43012
  429.9 442.4 %all-reduce.5.cloned.1.call-start = ((), (), s32[]{:S(2)}) async-start(), calls=%async_computation.5 | async-start | bytes 5505024 | tf_op jit(solution)/shard_map/psum | solution.py:76
  676.0 6.6 copy-start
  791.4 83.4 %copy-start.6 = (f32[3584]{0:T(1024)S(1)}, f32[3584]{0:T(1024)}, u32[]{:S(2)}) copy-start(f32[3584]{0:T(1024)} %param.20) | copy-start | bytes 43012
  791.4 88.1 %copy-start.7 = (f32[3584]{0:T(1024)S(1)}, f32[3584]{0:T(1024)}, u32[]{:S(2)}) copy-start(f32[3584]{0:T(1024)} %param.21) | copy-start | bytes 43012
  872.2 7.4 copy-start.1
  872.2 7.4 copy-start.2
Sparse Core Ops, SparseCore 0:
  16.1 226.8 all-gather.7
  339.1 36.9 all-gather.3
  377.8 37.0 all-gather.5
  430.0 245.9 all-reduce.2
  791.5 80.6 all-reduce.4
where the time goes:
time: 907 us; the launch traced here: 898 us
  waiting for transfers between devices  583 us (64%)
  local copies, waits for them, and re-layouts  165 us (18%)
  matrix products  73.5 us (8%)
  other arithmetic  40.9 us (5%)
  starting transfers between devices  22 us (2%)
  between operations  13.5 us (1%)
    psum x2, waiting for transfers between devices, total_of(): return lax.psum(values.astype(jnp.bfloat16), 'tp').astype(jnp.float32)  314 us
    all_gather x1, waiting for transfers between devices, local(): stacked_rows = lax.all_gather(server_low, 'seq', axis=1, tiled=True)  227 us
    all_gather x1, local copies, waits for them, and re-layouts, local(): stacked_rows = lax.all_gather(server_low, 'seq', axis=1, tiled=True)  84.6 us
    all_gather x1, waiting for transfers between devices, local(): lax.all_gather(own_keys, 'seq', axis=0, tiled=True)  34.1 us
    slice x2, local copies, waits for them, and re-layouts, local(): local_units[0]  26.8 us
    dot_general x1, matrix products, local(): jnp.dot(activated, down_weight, preferred_element_type=jnp.float32)  23.1 us
    sub x1, other arithmetic, local(): weights = jnp.where(allowed, jnp.exp(scores - peak), 0.0)  20.2 us
  transfers between devices with their start and end apart: 6, of which 5 were waited for; matrix products, arithmetic and copies ran while one was open for 8% of the time, Pallas kernels for 0%

commit v1 on v0

v1 whole, which is shorter than its diff:
```python
import functools

import jax
import jax.numpy as jnp
from jax import lax
from jax.experimental import pallas as pl
from jax.experimental.pallas import tpu as pltpu
from jax.sharding import PartitionSpec as P

HEADS = 16
KV_HEADS = 8
HEAD_DIM = 256
PER_GROUP = HEADS // KV_HEADS
GROUP_COLS = (PER_GROUP + 2) * HEAD_DIM
MIB = 1 << 20


def rms_norm(values, gain):
    meansq = jnp.mean(values * values, axis=-1, keepdims=True)
    return values * lax.rsqrt(meansq + 1e-06) * gain


def tp_swap(values, bits):
    size = lax.axis_size("tp")
    return lax.ppermute(values, "tp", [(i, i ^ bits) for i in range(size)])


def seq_swap(values, bits):
    size = lax.axis_size("seq")
    return lax.ppermute(values, "seq", [(i, i ^ bits) for i in range(size)])


def seq_up(values):
    size = lax.axis_size("seq")
    return lax.ppermute(values, "seq", [(i, i + 2) for i in range(size - 2)])


def attention_kernel(ends_ref, place_ref, joined_ref, *refs, block_count, prompts, parts):
    kv_refs = refs[:block_count]
    out_ref, peak, total, acc = refs[block_count:]
    rows = joined_ref.shape[0]
    piece = rows // parts
    first = place_ref[1]
    queries = jnp.concatenate(
        [joined_ref[:, r * HEAD_DIM : (r + 1) * HEAD_DIM] for r in range(PER_GROUP)], axis=0
    )
    stacked = PER_GROUP * rows
    at = first + lax.rem(lax.broadcasted_iota(jnp.int32, (stacked, 1), 0), rows)
    start = jnp.zeros_like(at)
    lowest = jnp.int32(0)
    for p in range(prompts):
        end = ends_ref[p]
        start = jnp.where(at >= end, jnp.maximum(start, end), start)
        lowest = jnp.where(first >= end, jnp.maximum(lowest, end), lowest)

    def scores_of(keys, base):
        scores = lax.dot_general(
            queries, keys, (((1,), (1,)), ((), ())), preferred_element_type=jnp.float32
        ) * (HEAD_DIM ** (-0.5))
        places = base + lax.broadcasted_iota(jnp.int32, (1, rows), 1)
        return jnp.where((places >= start) & (places <= at), scores, -1e30)

    own_keys = joined_ref[:, PER_GROUP * HEAD_DIM : (PER_GROUP + 1) * HEAD_DIM]
    own_values = joined_ref[:, (PER_GROUP + 1) * HEAD_DIM :]
    scores = scores_of(own_keys, first)
    top = jnp.max(scores, axis=1, keepdims=True)
    weights = jnp.exp(scores - top)
    peak[...] = jnp.broadcast_to(top, peak.shape)
    total[...] = jnp.broadcast_to(jnp.sum(weights, axis=1, keepdims=True), total.shape)
    acc[...] = jnp.dot(
        weights.astype(jnp.bfloat16), own_values, preferred_element_type=jnp.float32
    )
    for i in range(block_count):
        base = place_ref[2 + i]

        @pl.when((base >= 0) & (base + rows > lowest) & (base < first))
        def _(i=i, base=base):
            scores = scores_of(kv_refs[i][:, :HEAD_DIM], base)
            before = peak[:, :1]
            top = jnp.maximum(before, jnp.max(scores, axis=1, keepdims=True))
            weights = jnp.exp(scores - top)
            shrink = jnp.exp(before - top)
            peak[...] = jnp.broadcast_to(top, peak.shape)
            total[...] = total[...] * shrink + jnp.sum(weights, axis=1, keepdims=True)
            acc[...] = acc[...] * shrink + jnp.dot(
                weights.astype(jnp.bfloat16),
                kv_refs[i][:, HEAD_DIM:],
                preferred_element_type=jnp.float32,
            )

    result = (acc[...] / total[:, :1]).astype(jnp.bfloat16)
    for j in range(parts):
        to = pl.multiple_of((place_ref[0] ^ j) * piece, piece)
        for r in range(PER_GROUP):
            out_ref[pl.ds(to, piece), r * HEAD_DIM : (r + 1) * HEAD_DIM] = result[
                r * rows + j * piece : r * rows + (j + 1) * piece
            ]


def attend(joined, kv_blocks, bases, ends, tp_index, first, parts):
    rows, cols = joined.shape
    groups = cols // GROUP_COLS
    place = jnp.stack([tp_index, first] + bases).astype(jnp.int32)
    count = len(kv_blocks)
    stacked = PER_GROUP * rows
    return pl.pallas_call(
        functools.partial(
            attention_kernel, block_count=count, prompts=ends.shape[0], parts=parts
        ),
        grid_spec=pltpu.PrefetchScalarGridSpec(
            num_scalar_prefetch=2,
            grid=(groups,),
            in_specs=[pl.BlockSpec((rows, GROUP_COLS), lambda g, *_: (0, g))]
            + [pl.BlockSpec((rows, 2 * HEAD_DIM), lambda g, *_: (0, g))] * count,
            out_specs=pl.BlockSpec((rows, PER_GROUP * HEAD_DIM), lambda g, *_: (0, g)),
            scratch_shapes=[
                pltpu.VMEM((stacked, 128), jnp.float32),
                pltpu.VMEM((stacked, 128), jnp.float32),
                pltpu.VMEM((stacked, HEAD_DIM), jnp.float32),
            ],
        ),
        out_shape=jax.ShapeDtypeStruct((rows, groups * PER_GROUP * HEAD_DIM), jnp.bfloat16),
        compiler_params=pltpu.CompilerParams(vmem_limit_bytes=48 * MIB),
        cost_estimate=pl.CostEstimate(
            flops=groups * 4 * stacked * rows * HEAD_DIM * (count + 1),
            bytes_accessed=rows * cols * 2 + count * rows * groups * HEAD_DIM * 4,
            transcendentals=groups * stacked * rows * (count + 1),
        ),
        name="attention",
    )(ends, place, joined, *kv_blocks)


def gate_up_kernel(place_ref, *refs, parts, buffers, subs):
    x_refs, w_refs = refs[:parts], refs[parts : parts + buffers]
    out_ref, x_all, w_all, acc, sems = refs[parts + buffers :]
    piece = x_refs[0].shape[0]
    depth, both = w_all.shape
    hidden = both // 2
    sub_rows = w_refs[0].shape[1]

    def copies(i):
        found = []
        for k in range(subs):
            to = pl.multiple_of(place_ref[1 + i * subs + k], 16)
            found.append(
                pltpu.make_async_copy(
                    w_refs[i].at[k], w_all.at[pl.ds(to, sub_rows)], sems.at[i * subs + k]
                )
            )
        return found

    for i in range(buffers):
        for copy in copies(i):
            copy.start()
    for k in range(parts):
        x_all[k * piece : (k + 1) * piece] = x_refs[k][...]
    half_depth = depth // 2
    tile = 256 if both % 256 == 0 else 128
    for part in range(2):
        for i in range(part * buffers // 2, (part + 1) * buffers // 2):
            for copy in copies(i):
                copy.wait()
        half = place_ref[0] ^ part
        from_row = pl.multiple_of(half * half_depth, 128)

        @pl.loop(0, both // tile)
        def _(j, part=part, from_row=from_row):
            at = pl.ds(pl.multiple_of(j * tile, tile), tile)
            product = jnp.dot(
                x_all[:, pl.ds(from_row, half_depth)],
                w_all[pl.ds(from_row, half_depth), at],
                preferred_element_type=jnp.float32,
            )
            if part == 0:
                acc[:, at] = product
            else:
                acc[:, at] += product

    out_ref[...] = (
        jax.nn.gelu(acc[:, :hidden], approximate=True) * acc[:, hidden:]
    ).astype(jnp.bfloat16)


def gate_up_act(x_pieces, weights, offsets, half):
    parts, buffers = len(x_pieces), len(weights)
    subs = weights[0].shape[0]
    hidden = weights[0].shape[2] // 2
    piece, depth = x_pieces[0].shape
    rows = parts * piece
    place = jnp.stack([half] + offsets).astype(jnp.int32)
    return pl.pallas_call(
        functools.partial(gate_up_kernel, parts=parts, buffers=buffers, subs=subs),
        in_specs=[pl.BlockSpec(memory_space=pltpu.SMEM)]
        + [pl.BlockSpec(memory_space=pltpu.VMEM)] * parts
        + [pl.BlockSpec(memory_space=pl.ANY)] * buffers,
        out_specs=pl.BlockSpec(memory_space=pltpu.VMEM),
        out_shape=jax.ShapeDtypeStruct((rows, hidden), jnp.bfloat16),
        scratch_shapes=[
            pltpu.VMEM((rows, depth), jnp.bfloat16),
            pltpu.VMEM((depth, 2 * hidden), jnp.bfloat16),
            pltpu.VMEM((rows, 2 * hidden), jnp.float32),
            pltpu.SemaphoreType.DMA((buffers * subs,)),
        ],
        compiler_params=pltpu.CompilerParams(vmem_limit_bytes=48 * MIB),
        cost_estimate=pl.CostEstimate(
            flops=4 * rows * depth * hidden,
            bytes_accessed=depth * hidden * 4 + rows * depth * 2,
            transcendentals=rows * hidden,
        ),
        name="gate_up",
    )(place, *x_pieces, *weights)


def gather_weights(gate_up, tp_index, seq_index):
    seq_count, tp_count = lax.axis_size("seq"), lax.axis_size("tp")
    half_count = seq_count // 2
    half = seq_index // half_count
    piece_rows = gate_up.shape[1]
    units = gate_up.shape[2] // tp_count
    hidden = units // 2
    pieces = []
    for k in range(tp_count):
        cut = lax.dynamic_slice(
            gate_up, (0, 0, (tp_index ^ k) * units), (2, piece_rows, units)
        ).astype(jnp.bfloat16)
        pieces.append(tp_swap(cut, k) if k else cut)

    def columns(which):
        cuts = [lax.dynamic_slice_in_dim(p, which * hidden, hidden, 2) for p in pieces]
        cuts = [jnp.concatenate([cut[0], cut[1]], axis=1) for cut in cuts]
        stack = jnp.stack(cuts)
        if piece_rows % 16 == 0:
            return stack
        ordered = [
            lax.dynamic_index_in_dim(stack, tp_index ^ j, 0, keepdims=False)
            for j in range(tp_count)
        ]
        return jnp.concatenate(ordered, axis=0)[None]

    mine, other = columns(half), columns(1 - half)
    found = {0: mine, half_count: seq_swap(other, half_count)}
    bits = 2
    while bits < half_count:
        for key in list(found):
            found[key ^ bits] = seq_swap(found[key], bits)
        bits *= 2
    for key in list(found):
        found[key ^ 1] = seq_swap(found[key], 1)
    keys = sorted(found)
    subs, sub_rows = mine.shape[0], mine.shape[1]
    offsets = []
    for key in keys:
        base = (seq_index ^ key) * (tp_count * piece_rows)
        for k in range(subs):
            offsets.append(base + (tp_index ^ k) * sub_rows if subs > 1 else base)
    return [found[key] for key in keys], offsets, half


def tp_total(partial, parts):
    piece = partial.shape[0] // parts
    total = partial[:piece].astype(jnp.float32)
    for k in range(1, parts):
        total = total + tp_swap(partial[k * piece : (k + 1) * piece], k).astype(jnp.float32)
    return total


def tp_gather(values, parts):
    return [values] + [tp_swap(values, k) for k in range(1, parts)]


def local(
    hidden_in,
    joined_inputs,
    lengths,
    o_weight,
    gate_up,
    down_weight,
    next_weight,
    post_attn_gain,
    pre_ffw_gain,
    post_ffw_gain,
    next_gain,
):
    seq_count, tp_count = lax.axis_size("seq"), lax.axis_size("tp")
    seq_index, tp_index = lax.axis_index("seq"), lax.axis_index("tp")
    rows = hidden_in.shape[0]
    piece = rows // tp_count
    half_count = seq_count // 2
    groups = joined_inputs.shape[1] // GROUP_COLS

    own_kv = jnp.concatenate(
        [
            joined_inputs[:, g * GROUP_COLS + PER_GROUP * HEAD_DIM : (g + 1) * GROUP_COLS]
            for g in range(groups)
        ],
        axis=1,
    )
    chain = [own_kv]
    for _ in range(seq_count // 4):
        chain.append(seq_up(chain[-1]))
    other = [seq_swap(block, 1) for block in chain]
    blocks, bases = [], []
    for j in range(len(chain)):
        if j:
            blocks.append(chain[j])
            bases.append((seq_index - 2 * j) * rows)
        blocks.append(other[j])
        bases.append(((seq_index ^ 1) - 2 * j) * rows)

    weights, offsets, half = gather_weights(gate_up, tp_index, seq_index)

    ends = jnp.cumsum(lengths).astype(jnp.int32)
    attended = attend(
        joined_inputs, blocks, bases, ends, tp_index, seq_index * rows, tp_count
    )
    projected = jnp.dot(attended, o_weight, preferred_element_type=jnp.float32).astype(
        jnp.bfloat16
    )
    hidden_piece = lax.dynamic_slice_in_dim(hidden_in, tp_index * piece, piece, 0)
    residual_mid = hidden_piece.astype(jnp.float32) + rms_norm(
        tp_total(projected, tp_count), post_attn_gain
    )
    ffw_in = rms_norm(residual_mid, pre_ffw_gain).astype(jnp.bfloat16)
    partner_in = seq_swap(ffw_in, half_count)
    own_act = gate_up_act(tp_gather(ffw_in, tp_count), weights, offsets, half)
    partner_act = gate_up_act(tp_gather(partner_in, tp_count), weights, offsets, half)
    returned = seq_swap(partner_act, half_count)
    activated = jnp.where(
        half == 0,
        jnp.concatenate([own_act, returned], axis=1),
        jnp.concatenate([returned, own_act], axis=1),
    )
    ffw_out = jnp.dot(activated, down_weight, preferred_element_type=jnp.float32).astype(
        jnp.bfloat16
    )
    residual_out = residual_mid + rms_norm(tp_total(ffw_out, tp_count), post_ffw_gain)
    next_in = rms_norm(residual_out, next_gain).astype(jnp.bfloat16)
    next_all = jnp.concatenate(tp_gather(next_in, tp_count), axis=0)
    result = jnp.dot(next_all, next_weight, preferred_element_type=jnp.float32).astype(
        jnp.bfloat16
    )
    return jnp.concatenate(
        [
            lax.dynamic_slice_in_dim(result, (tp_index ^ j) * piece, piece, 0)
            for j in range(tp_count)
        ],
        axis=0,
    )


def solution(mesh):
    in_specs = (
        P("seq", None),
        P("seq", "tp"),
        P(),
        P("tp", None),
        P(None, ("seq", "tp"), None),
        P("tp", None),
        P(None, "tp"),
        P(),
        P(),
        P(),
        P(),
    )
    out_specs = P("seq", "tp")
    return jax.shard_map(local, mesh=mesh, in_specs=in_specs, out_specs=out_specs, check_vma=False)
```

time: 907 us -> 362 us (0.40)
  waiting for transfers between devices: 583 us -> 241 us
  local copies, waits for them, and re-layouts: 165 us -> 10.2 us
  matrix products: 73.5 us -> 25.8 us
  other arithmetic: 40.9 us -> 8.72 us
  Pallas kernels: 0 us -> 31.4 us
  starting transfers between devices: 22 us -> 45 us
  between operations: 13.5 us -> 0.37 us
    psum x2 -> x0, waiting for transfers between devices: 314 us -> none  [total_of(): return lax.psum(values.astype(jnp.bfloat16), 'tp').astype(jnp.float32)]
    all_gather x3 -> x0, waiting for transfers between devices: 268 us -> none  [the longest x1 227 us: local(): stacked_rows = lax.all_gather(server_low, 'seq', axis=1, tiled=True)]
    ppermute x0 -> x32, waiting for transfers between devices: none -> 241 us  [the longest x12 120 us: seq_swap(): return lax.ppermute(values, 'seq', [(i, i ^ bits) for i in range(size)])]
    all_gather x1 -> x0, local copies, waits for them, and re-layouts: 84.6 us -> none  [local(): stacked_rows = lax.all_gather(server_low, 'seq', axis=1, tiled=True)]
    ppermute x0 -> x32, starting transfers between devices: none -> 45 us  [the longest x18 27.7 us: tp_swap(): return lax.ppermute(values, 'tp', [(i, i ^ bits) for i in range(size)])]
    slice x5 -> x3, local copies, waits for them, and re-layouts: 45.6 us -> 1.66 us  [the longest x2 1.59 us: tp_total(): partial[k * piece:(k + 1) * piece]]
    dot_general x5 -> x2, matrix products: 50.4 us -> 15.4 us  [the longest x1 9.12 us: local(): jnp.dot(next_all, next_weight, preferred_element_type=jnp.float32)]
    pallas_call x0 -> x3, Pallas kernels: none -> 31.4 us  [the longest x2 26.8 us: gate_up_act(): pl.pallas_call(functools.partial(gate_up_kernel, parts=parts, buffers=buf...]
  transfers between devices with their start and end apart: 6 -> 32, of which waited for: 5 -> 16; matrix products, arithmetic and copies ran while one was open for 8% -> 4% of each run, Pallas kernels for 0% -> 9%
where the time goes in v1:
time: 362 us
  waiting for transfers between devices  241 us (67%)
  starting transfers between devices  45 us (12%)
  Pallas kernels  31.4 us (9%)
  matrix products  25.8 us (7%)
  local copies, waits for them, and re-layouts  10.2 us (3%)
  other arithmetic  8.72 us (2%)
    ppermute x12, waiting for transfers between devices, seq_swap(): return lax.ppermute(values, 'seq', [(i, i ^ bits) for i in range(size)])  120 us
    ppermute x18, waiting for transfers between devices, tp_swap(): return lax.ppermute(values, 'tp', [(i, i ^ bits) for i in range(size)])  101 us
    ppermute x18, starting transfers between devices, tp_swap(): return lax.ppermute(values, 'tp', [(i, i ^ bits) for i in range(size)])  27.7 us
    pallas_call x2, Pallas kernels, gate_up_act(): pl.pallas_call(functools.partial(gate_up_kernel, parts=parts, buffers=buf...  26.8 us
    ppermute x2, waiting for transfers between devices, seq_up(): return lax.ppermute(values, 'seq', [(i, i + 2) for i in range(size - 2)])  19.9 us
    dot_general x1, matrix products, local(): jnp.dot(activated, down_weight, preferred_element_type=jnp.float32)  10.3 us
    ppermute x12, starting transfers between devices, seq_swap(): return lax.ppermute(values, 'seq', [(i, i ^ bits) for i in range(size)])  9.5 us
    dot_general x1, matrix products, local(): jnp.dot(next_all, next_weight, preferred_element_type=jnp.float32)  9.12 us
  transfers between devices with their start and end apart: 32, of which 16 were waited for; matrix products, arithmetic and copies ran while one was open for 4% of the time, Pallas kernels for 9%

profile of v1, /device:TPU:0, one launch (start us, length us, event | category | flops | bytes accessed | tf_op | source)
XLA Modules:
  0.0 362.1 jit_solution(10826478464966547739)
XLA Ops:
  0.0 4.5 %dynamic-slice_convert_fusion.3 = (bf16[2,112,1792]{2,1,0:T(8,128)(2,1)S(1)}, bf16[2,112,1792]{2,1,0:T(8,128)(2,1)}, bf16[2,112,1792]{2,1,0:T(8,128)(2,1)}, bf16[2,112,1792]{2,1,0:T(8,128)(2,1)}) fusion(f32[2,112,7168]{2,1,0:T(8,128)} %param.15, s32[]{:T(128)S(6)} %select_n.53, s32[]{:T(128)S(6)} %select_n.55, s32[]{:T(128)S(6)} %select_n.57, s32[]{:T(128)S(6)} %select_n.56), kind=kLoop, calls=%fused_computation.15 | loop fusion | bytes 6422544 | tf_op jit(solution)/shard_map/convert_element_type | solution.py:225
  4.5 3.9 %collective-permute-start.13 = (bf16[2,112,1792]{2,1,0:T(8,128)(2,1)}, bf16[2,112,1792]{2,1,0:T(8,128)(2,1)}, u32[]{:S(2)}, u32[]{:S(2)}) collective-permute-start(bf16[2,112,1792]{2,1,0:T(8,128)(2,1)} %get-tuple-element.11), channel_id=1, source_target_pairs={{0,3},{1,2},{2,1},{3,0},{4,7},{5,6},{6,5},{7,4},{8,11},{9,10},{10,... | collective-permute-start | bytes 2408456 | tf_op jit(solution)/shard_map/ppermute | solution.py:25
  14.4 15.5 %collective-permute-done.1.refs_1_ = bf16[384,1024]{1,0:T(8,128)(2,1)S(1)} collective-permute-done((bf16[384,1024]{1,0:T(8,128)(2,1)}, bf16[384,1024]{1,0:T(8,128)(2,1)S(1)}, u32[]{:S(2)}, u32[]{:S(2)}) %collective-permute-start.1) | collective-permute-done | bytes 786464 | tf_op jit(solution)/shard_map/ppermute | solution.py:35
  30.0 4.3 %collective-permute-start.3 = (bf16[384,1024]{1,0:T(8,128)(2,1)S(1)}, bf16[384,1024]{1,0:T(8,128)(2,1)S(1)}, u32[]{:S(2)}, u32[]{:S(2)}) collective-permute-start(bf16[384,1024]{1,0:T(8,128)(2,1)S(1)} %collective-permute-done.1.refs_1_), channel_id=1, source_target_pairs={{0,8},{4,12},{8,16},{12,20},{16,24},{20,28},{1,9},{5,13},{9,17},{1... | collective-permute-start | bytes 2359304 | tf_op jit(solution)/shard_map/ppermute | solution.py:35
  34.3 9.5 %collective-permute-done.12 = bf16[2,112,1792]{2,1,0:T(8,128)(2,1)} collective-permute-done((bf16[2,112,1792]{2,1,0:T(8,128)(2,1)}, bf16[2,112,1792]{2,1,0:T(8,128)(2,1)}, u32[]{:S(2)}, u32[]{:S(2)}) %collective-permute-start.12) | collective-permute-done | bytes 802848 | tf_op jit(solution)/shard_map/ppermute | solution.py:25
  47.7 4.4 %collective-permute-done.3.refs_3_ = bf16[384,1024]{1,0:T(8,128)(2,1)S(1)} collective-permute-done((bf16[384,1024]{1,0:T(8,128)(2,1)S(1)}, bf16[384,1024]{1,0:T(8,128)(2,1)S(1)}, u32[]{:S(2)}, u32[]{:S(2)}) %collective-permute-start.3) | collective-permute-done | bytes 786464 | tf_op jit(solution)/shard_map/ppermute | solution.py:35
  55.6 4.5 %attention.1 = bf16[384,1024]{1,0:T(8,128)(2,1)S(1)} custom-call(s32[4]{0:T(128)S(1)} %bitcast.94, s32[7]{0:T(128)S(1)} %stack.197.place_ref, bf16[384,2048]{1,0:T(8,128)(2,1)} %joined_ref.1, bf16[384,1024]{1,0:T(8,128)(2,1)S(1)} %collective-permute-done.refs_0_, bf16[384,1024]{1,0:T(8,128)(2,1)S(1)} %collective-permute-done.1.refs_1_, ...), custom_call_target="tpu_custom_call" | custom-call | flops 3623878656 | bytes 5505024 | tf_op jit(solution)/shard_map/attention/pallas_call | solution.py:106
  60.2 6.3 %convolution_convert_fusion.1 = bf16[384,3584]{1,0:T(8,128)(2,1)S(1)} fusion(bf16[384,1024]{1,0:T(8,128)(2,1)S(1)} %attention.1, bf16[1024,3584]{1,0:T(8,128)(2,1)} %param.14), kind=kOutput, calls=%fused_computation.1 | convolution fusion | flops 2819948544 | bytes 10878976 | tf_op jit(solution)/shard_map/dot_general | solution.py:316
  72.2 53.7 %collective-permute-done.17.refs_8_ = bf16[4,112,1792]{2,1,0:T(8,128)(2,1)} collective-permute-done((bf16[4,112,1792]{2,1,0:T(8,128)(2,1)S(1)}, bf16[4,112,1792]{2,1,0:T(8,128)(2,1)}, u32[]{:S(2)}, u32[]{:S(2)}) %collective-permute-start.17) | collective-permute-done | bytes 1605664 | tf_op jit(solution)/shard_map/ppermute | solution.py:30
  131.8 31.4 %collective-permute-done.19.refs_10_ = bf16[4,112,1792]{2,1,0:T(8,128)(2,1)} collective-permute-done((bf16[4,112,1792]{2,1,0:T(8,128)(2,1)}, bf16[4,112,1792]{2,1,0:T(8,128)(2,1)}, u32[]{:S(2)}, u32[]{:S(2)}) %collective-permute-start.19) | collective-permute-done | bytes 1605664 | tf_op jit(solution)/shard_map/ppermute | solution.py:30
  166.1 30.9 %collective-permute-done.21.refs_0_ = bf16[96,3584]{1,0:T(8,128)(2,1)S(1)} collective-permute-done((bf16[96,3584]{1,0:T(8,128)(2,1)S(1)}, bf16[96,3584]{1,0:T(8,128)(2,1)S(1)}, u32[]{:S(2)}, u32[]{:S(2)}) %collective-permute-start.21) | collective-permute-done | bytes 688160 | tf_op jit(solution)/shard_map/ppermute | solution.py:30
  203.1 12.3 %collective-permute-done.22.refs_1_ = bf16[96,3584]{1,0:T(8,128)(2,1)} collective-permute-done((bf16[96,3584]{1,0:T(8,128)(2,1)S(1)}, bf16[96,3584]{1,0:T(8,128)(2,1)}, u32[]{:S(2)}, u32[]{:S(2)}) %collective-permute-start.22) | collective-permute-done | bytes 688160 | tf_op jit(solution)/shard_map/ppermute | solution.py:25
  216.9 10.0 %collective-permute-done.23.refs_2_ = bf16[96,3584]{1,0:T(8,128)(2,1)} collective-permute-done((bf16[96,3584]{1,0:T(8,128)(2,1)S(1)}, bf16[96,3584]{1,0:T(8,128)(2,1)}, u32[]{:S(2)}, u32[]{:S(2)}) %collective-permute-start.23) | collective-permute-done | bytes 688160 | tf_op jit(solution)/shard_map/ppermute | solution.py:25
  227.0 5.8 %collective-permute-start.10 = (bf16[96,3584]{1,0:T(8,128)(2,1)S(1)}, bf16[96,3584]{1,0:T(8,128)(2,1)}, u32[]{:S(2)}, u32[]{:S(2)}) collective-permute-start(bf16[96,3584]{1,0:T(8,128)(2,1)S(1)} %multiply_convert_fusion.1.refs_0_), channel_id=1, source_target_pairs={{0,3},{1,2},{2,1},{3,0},{4,7},{5,6},{6,5},{7,4},{8,11},{9,10},{10,... | collective-permute-start | bytes 2064392 | tf_op jit(solution)/shard_map/ppermute | solution.py:25
  232.7 14.0 %gate_up.3 = bf16[384,896]{1,0:T(8,128)(2,1)} custom-call(s32[33]{0:T(128)S(1)} %stack.231.place_ref, bf16[96,3584]{1,0:T(8,128)(2,1)S(1)} %collective-permute-done.21.refs_0_, bf16[96,3584]{1,0:T(8,128)(2,1)} %collective-permute-done.22.refs_1_, bf16[96,3584]{1,0:T(8,128)(2,1)} %collective-permute-done.23.refs_2_, ...), custom_call_target="tpu_custom_call" | custom-call | flops 4932501504 | bytes 15597568 | tf_op jit(solution)/shard_map/gate_up/pallas_call | solution.py:191
  246.8 10.8 %collective-permute-done.9.refs_2_ = bf16[96,3584]{1,0:T(8,128)(2,1)} collective-permute-done((bf16[96,3584]{1,0:T(8,128)(2,1)S(1)}, bf16[96,3584]{1,0:T(8,128)(2,1)}, u32[]{:S(2)}, u32[]{:S(2)}) %collective-permute-start.9) | collective-permute-done | bytes 688160 | tf_op jit(solution)/shard_map/ppermute | solution.py:25
  259.4 12.9 %gate_up.2 = bf16[384,896]{1,0:T(8,128)(2,1)S(1)} custom-call(s32[33]{0:T(128)S(1)} %stack.231.place_ref, bf16[96,3584]{1,0:T(8,128)(2,1)S(1)} %multiply_convert_fusion.1.refs_0_, bf16[96,3584]{1,0:T(8,128)(2,1)} %collective-permute-done.8.refs_1_, bf16[96,3584]{1,0:T(8,128)(2,1)} %collective-permute-done.9.refs_2_, ...), custom_call_target="tpu_custom_call" | custom-call | flops 4932501504 | bytes 15597568 | tf_op jit(solution)/shard_map/gate_up/pallas_call | solution.py:191
  272.3 3.8 %collective-permute-done.25 = bf16[384,896]{1,0:T(8,128)(2,1)} collective-permute-done((bf16[384,896]{1,0:T(8,128)(2,1)}, bf16[384,896]{1,0:T(8,128)(2,1)}, u32[]{:S(2)}, u32[]{:S(2)}) %collective-permute-start.25) | collective-permute-done | bytes 688160 | tf_op jit(solution)/shard_map/ppermute | solution.py:30
  276.1 10.3 %convolution_convert_fusion = bf16[384,3584]{1,0:T(8,128)(2,1)S(1)} fusion(bf16[1792,3584]{1,0:T(8,128)(2,1)} %param.16, bf16[384,896]{1,0:T(8,128)(2,1)} %collective-permute-done.25, bf16[384,896]{1,0:T(8,128)(2,1)S(1)} %gate_up.2, pred[]{:T(512)S(6)} %eq.3), kind=kOutput, calls=%fused_computation | convolution fusion | flops 4940070912 | bytes 16973824 | tf_op jit(solution)/shard_map/dot_general | solution.py:333
  290.2 15.8 %collective-permute-done.28 = bf16[96,3584]{1,0:T(8,128)(2,1)S(1)} collective-permute-done((bf16[96,3584]{1,0:T(8,128)(2,1)S(1)}, bf16[96,3584]{1,0:T(8,128)(2,1)S(1)}, u32[]{:S(2)}, u32[]{:S(2)}) %collective-permute-start.28) | collective-permute-done | bytes 688160 | tf_op jit(solution)/shard_map/ppermute | solution.py:25
  306.0 11.4 %collective-permute-done.27 = bf16[96,3584]{1,0:T(8,128)(2,1)S(1)} collective-permute-done((bf16[96,3584]{1,0:T(8,128)(2,1)S(1)}, bf16[96,3584]{1,0:T(8,128)(2,1)S(1)}, u32[]{:S(2)}, u32[]{:S(2)}) %collective-permute-start.27) | collective-permute-done | bytes 688160 | tf_op jit(solution)/shard_map/ppermute | solution.py:25
  322.4 15.8 %collective-permute-done.31 = bf16[96,3584]{1,0:T(8,128)(2,1)S(1)} collective-permute-done((bf16[96,3584]{1,0:T(8,128)(2,1)S(1)}, bf16[96,3584]{1,0:T(8,128)(2,1)S(1)}, u32[]{:S(2)}, u32[]{:S(2)}) %collective-permute-start.31) | collective-permute-done | bytes 688160 | tf_op jit(solution)/shard_map/ppermute | solution.py:25
  338.2 12.9 %collective-permute-done.30 = bf16[96,3584]{1,0:T(8,128)(2,1)S(1)} collective-permute-done((bf16[96,3584]{1,0:T(8,128)(2,1)S(1)}, bf16[96,3584]{1,0:T(8,128)(2,1)S(1)}, u32[]{:S(2)}, u32[]{:S(2)}) %collective-permute-start.30) | collective-permute-done | bytes 688160 | tf_op jit(solution)/shard_map/ppermute | solution.py:25
  351.6 9.1 %convolution_convert_fusion.2 = bf16[384,2048]{1,0:T(8,128)(2,1)S(1)} fusion(bf16[3584,2048]{1,0:T(8,128)(2,1)} %param.17, bf16[96,3584]{1,0:T(8,128)(2,1)S(1)} %collective-permute-done.31, bf16[96,3584]{1,0:T(8,128)(2,1)S(1)} %collective-permute-done.30, bf16[96,3584]{1,0:T(8,128)(2,1)S(1)} %collective-permute-done.29, ...), kind=kOutput, calls=%fused_computation.2 | convolution fusion | flops 5648941056 | bytes 19005440 | tf_op jit(solution)/shard_map/dot_general | solution.py:339
  (99 shorter events, 47.8 us)
Async XLA Ops:
  8.4 35.4 %collective-permute-start.12 = (bf16[2,112,1792]{2,1,0:T(8,128)(2,1)}, bf16[2,112,1792]{2,1,0:T(8,128)(2,1)}, u32[]{:S(2)}, u32[]{:S(2)}) collective-permute-start(bf16[2,112,1792]{2,1,0:T(8,128)(2,1)} %get-tuple-element.12), channel_id=1, source_target_pairs={{0,2},{1,3},{2,0},{3,1},{4,6},{5,7},{6,4},{7,5},{8,10},{9,11},{10,... | collective-permute-start | bytes 2408456 | tf_op jit(solution)/shard_map/ppermute | solution.py:25
  13.5 32.0 %collective-permute-start.11 = (bf16[2,112,1792]{2,1,0:T(8,128)(2,1)}, bf16[2,112,1792]{2,1,0:T(8,128)(2,1)S(1)}, u32[]{:S(2)}, u32[]{:S(2)}) collective-permute-start(bf16[2,112,1792]{2,1,0:T(8,128)(2,1)} %get-tuple-element.10), channel_id=1, source_target_pairs={{0,1},{1,0},{2,3},{3,2},{4,5},{5,4},{6,7},{7,6},{8,9},{9,8},{10,11... | collective-permute-start | bytes 2408456 | tf_op jit(solution)/shard_map/ppermute | solution.py:25
  14.1 41.5 %collective-permute-start = (bf16[384,1024]{1,0:T(8,128)(2,1)}, bf16[384,1024]{1,0:T(8,128)(2,1)S(1)}, u32[]{:S(2)}, u32[]{:S(2)}) collective-permute-start(bf16[384,1024]{1,0:T(8,128)(2,1)} %pad_maximum_fusion.3), channel_id=1, source_target_pairs={{0,4},{4,0},{8,12},{12,8},{16,20},{20,16},{24,28},{28,24},{1,5},{5... | collective-permute-start | bytes 2359304 | tf_op jit(solution)/shard_map/ppermute | solution.py:30
  45.8 81.2 %collective-permute-start.15 = (bf16[4,112,1792]{2,1,0:T(8,128)(2,1)S(1)}, bf16[4,112,1792]{2,1,0:T(8,128)(2,1)}, u32[]{:S(2)}, u32[]{:S(2)}) collective-permute-start(bf16[4,112,1792]{2,1,0:T(8,128)(2,1)S(1)} %pad_maximum_fusion.refs_4_), channel_id=1, source_target_pairs={{0,8},{4,12},{8,0},{12,4},{16,24},{20,28},{24,16},{28,20},{1,9},{5... | collective-permute-start | bytes 4816904 | tf_op jit(solution)/shard_map/ppermute | solution.py:30
  52.4 73.5 %collective-permute-start.17 = (bf16[4,112,1792]{2,1,0:T(8,128)(2,1)S(1)}, bf16[4,112,1792]{2,1,0:T(8,128)(2,1)}, u32[]{:S(2)}, u32[]{:S(2)}) collective-permute-start(bf16[4,112,1792]{2,1,0:T(8,128)(2,1)S(1)} %pad_maximum_fusion.1), channel_id=1, source_target_pairs={{0,16},{4,20},{8,24},{12,28},{16,0},{20,4},{24,8},{28,12},{1,17},{... | collective-permute-start | bytes 4816904 | tf_op jit(solution)/shard_map/ppermute | solution.py:30
  68.7 58.3 %collective-permute-start.7 = (bf16[96,3584]{1,0:T(8,128)(2,1)}, bf16[96,3584]{1,0:T(8,128)(2,1)S(1)}, u32[]{:S(2)}, u32[]{:S(2)}) collective-permute-start(bf16[96,3584]{1,0:T(8,128)(2,1)} %get-tuple-element.17), channel_id=1, source_target_pairs={{0,3},{1,2},{2,1},{3,0},{4,7},{5,6},{6,5},{7,4},{8,11},{9,10},{10,... | collective-permute-start | bytes 2064392 | tf_op jit(solution)/shard_map/ppermute | solution.py:25
  70.2 57.4 %collective-permute-start.6 = (bf16[96,3584]{1,0:T(8,128)(2,1)}, bf16[96,3584]{1,0:T(8,128)(2,1)S(1)}, u32[]{:S(2)}, u32[]{:S(2)}) collective-permute-start(bf16[96,3584]{1,0:T(8,128)(2,1)} %get-tuple-element.18), channel_id=1, source_target_pairs={{0,2},{1,3},{2,0},{3,1},{4,6},{5,7},{6,4},{7,5},{8,10},{9,11},{10,... | collective-permute-start | bytes 2064392 | tf_op jit(solution)/shard_map/ppermute | solution.py:25
  70.7 56.9 %collective-permute-start.5 = (bf16[96,3584]{1,0:T(8,128)(2,1)}, bf16[96,3584]{1,0:T(8,128)(2,1)}, u32[]{:S(2)}, u32[]{:S(2)}) collective-permute-start(bf16[96,3584]{1,0:T(8,128)(2,1)} %get-tuple-element.16), channel_id=1, source_target_pairs={{0,1},{1,0},{2,3},{3,2},{4,5},{5,4},{6,7},{7,6},{8,9},{9,8},{10,11... | collective-permute-start | bytes 2064392 | tf_op jit(solution)/shard_map/ppermute | solution.py:25
  126.0 37.2 %collective-permute-start.19 = (bf16[4,112,1792]{2,1,0:T(8,128)(2,1)}, bf16[4,112,1792]{2,1,0:T(8,128)(2,1)}, u32[]{:S(2)}, u32[]{:S(2)}) collective-permute-start(bf16[4,112,1792]{2,1,0:T(8,128)(2,1)} %collective-permute-done.17.refs_8_), channel_id=1, source_target_pairs={{0,8},{4,12},{8,0},{12,4},{16,24},{20,28},{24,16},{28,20},{1,9},{5... | collective-permute-start | bytes 4816904 | tf_op jit(solution)/shard_map/ppermute | solution.py:30
  127.1 70.4 %collective-permute-start.14 = (bf16[4,112,1792]{2,1,0:T(8,128)(2,1)S(1)}, bf16[4,112,1792]{2,1,0:T(8,128)(2,1)S(1)}, u32[]{:S(2)}, u32[]{:S(2)}) collective-permute-start(bf16[4,112,1792]{2,1,0:T(8,128)(2,1)S(1)} %pad_maximum_fusion.refs_4_), channel_id=1, source_target_pairs={{0,4},{4,0},{8,12},{12,8},{16,20},{20,16},{24,28},{28,24},{1,5},{5... | collective-permute-start | bytes 4816904 | tf_op jit(solution)/shard_map/ppermute | solution.py:30
  127.1 75.4 %collective-permute-start.18 = (bf16[4,112,1792]{2,1,0:T(8,128)(2,1)}, bf16[4,112,1792]{2,1,0:T(8,128)(2,1)}, u32[]{:S(2)}, u32[]{:S(2)}) collective-permute-start(bf16[4,112,1792]{2,1,0:T(8,128)(2,1)} %collective-permute-done.17.refs_8_), channel_id=1, source_target_pairs={{0,4},{4,0},{8,12},{12,8},{16,20},{20,16},{24,28},{28,24},{1,5},{5... | collective-permute-start | bytes 4816904 | tf_op jit(solution)/shard_map/ppermute | solution.py:30
  127.6 71.5 %collective-permute-start.16 = (bf16[4,112,1792]{2,1,0:T(8,128)(2,1)}, bf16[4,112,1792]{2,1,0:T(8,128)(2,1)S(1)}, u32[]{:S(2)}, u32[]{:S(2)}) collective-permute-start(bf16[4,112,1792]{2,1,0:T(8,128)(2,1)} %collective-permute-done.15.refs_6_), channel_id=1, source_target_pairs={{0,4},{4,0},{8,12},{12,8},{16,20},{20,16},{24,28},{28,24},{1,5},{5... | collective-permute-start | bytes 4816904 | tf_op jit(solution)/shard_map/ppermute | solution.py:30
  163.2 69.5 %collective-permute-start.20 = (bf16[4,112,1792]{2,1,0:T(8,128)(2,1)}, bf16[4,112,1792]{2,1,0:T(8,128)(2,1)}, u32[]{:S(2)}, u32[]{:S(2)}) collective-permute-start(bf16[4,112,1792]{2,1,0:T(8,128)(2,1)} %collective-permute-done.19.refs_10_), channel_id=1, source_target_pairs={{0,4},{4,0},{8,12},{12,8},{16,20},{20,16},{24,28},{28,24},{1,5},{5... | collective-permute-start | bytes 4816904 | tf_op jit(solution)/shard_map/ppermute | solution.py:30
  163.4 33.6 %collective-permute-start.21 = (bf16[96,3584]{1,0:T(8,128)(2,1)S(1)}, bf16[96,3584]{1,0:T(8,128)(2,1)S(1)}, u32[]{:S(2)}, u32[]{:S(2)}) collective-permute-start(bf16[96,3584]{1,0:T(8,128)(2,1)S(1)} %multiply_convert_fusion.1.refs_0_), channel_id=1, source_target_pairs={{0,16},{4,20},{8,24},{12,28},{16,0},{20,4},{24,8},{28,12},{1,17},{... | collective-permute-start | bytes 2064392 | tf_op jit(solution)/shard_map/ppermute | solution.py:30
  197.5 29.5 %collective-permute-start.23 = (bf16[96,3584]{1,0:T(8,128)(2,1)S(1)}, bf16[96,3584]{1,0:T(8,128)(2,1)}, u32[]{:S(2)}, u32[]{:S(2)}) collective-permute-start(bf16[96,3584]{1,0:T(8,128)(2,1)S(1)} %collective-permute-done.21.refs_0_), channel_id=1, source_target_pairs={{0,2},{1,3},{2,0},{3,1},{4,6},{5,7},{6,4},{7,5},{8,10},{9,11},{10,... | collective-permute-start | bytes 2064392 | tf_op jit(solution)/shard_map/ppermute | solution.py:25
  200.2 32.5 %collective-permute-start.24 = (bf16[96,3584]{1,0:T(8,128)(2,1)S(1)}, bf16[96,3584]{1,0:T(8,128)(2,1)}, u32[]{:S(2)}, u32[]{:S(2)}) collective-permute-start(bf16[96,3584]{1,0:T(8,128)(2,1)S(1)} %collective-permute-done.21.refs_0_), channel_id=1, source_target_pairs={{0,3},{1,2},{2,1},{3,0},{4,7},{5,6},{6,5},{7,4},{8,11},{9,10},{10,... | collective-permute-start | bytes 2064392 | tf_op jit(solution)/shard_map/ppermute | solution.py:25
  202.5 44.3 %collective-permute-start.8 = (bf16[96,3584]{1,0:T(8,128)(2,1)S(1)}, bf16[96,3584]{1,0:T(8,128)(2,1)}, u32[]{:S(2)}, u32[]{:S(2)}) collective-permute-start(bf16[96,3584]{1,0:T(8,128)(2,1)S(1)} %multiply_convert_fusion.1.refs_0_), channel_id=1, source_target_pairs={{0,1},{1,0},{2,3},{3,2},{4,5},{5,4},{6,7},{7,6},{8,9},{9,8},{10,11... | collective-permute-start | bytes 2064392 | tf_op jit(solution)/shard_map/ppermute | solution.py:25
  215.4 42.2 %collective-permute-start.9 = (bf16[96,3584]{1,0:T(8,128)(2,1)S(1)}, bf16[96,3584]{1,0:T(8,128)(2,1)}, u32[]{:S(2)}, u32[]{:S(2)}) collective-permute-start(bf16[96,3584]{1,0:T(8,128)(2,1)S(1)} %multiply_convert_fusion.1.refs_0_), channel_id=1, source_target_pairs={{0,2},{1,3},{2,0},{3,1},{4,6},{5,7},{6,4},{7,5},{8,10},{9,11},{10,... | collective-permute-start | bytes 2064392 | tf_op jit(solution)/shard_map/ppermute | solution.py:25
  227.0 32.4 %collective-permute-start.10 = (bf16[96,3584]{1,0:T(8,128)(2,1)S(1)}, bf16[96,3584]{1,0:T(8,128)(2,1)}, u32[]{:S(2)}, u32[]{:S(2)}) collective-permute-start(bf16[96,3584]{1,0:T(8,128)(2,1)S(1)} %multiply_convert_fusion.1.refs_0_), channel_id=1, source_target_pairs={{0,3},{1,2},{2,1},{3,0},{4,7},{5,6},{6,5},{7,4},{8,11},{9,10},{10,... | collective-permute-start | bytes 2064392 | tf_op jit(solution)/shard_map/ppermute | solution.py:25
  246.7 29.4 %collective-permute-start.25 = (bf16[384,896]{1,0:T(8,128)(2,1)}, bf16[384,896]{1,0:T(8,128)(2,1)}, u32[]{:S(2)}, u32[]{:S(2)}) collective-permute-start(bf16[384,896]{1,0:T(8,128)(2,1)} %gate_up.3), channel_id=1, source_target_pairs={{0,16},{4,20},{8,24},{12,28},{16,0},{20,4},{24,8},{28,12},{1,17},{... | collective-permute-start | bytes 2064392 | tf_op jit(solution)/shard_map/ppermute | solution.py:30
  287.2 30.2 %collective-permute-start.27 = (bf16[96,3584]{1,0:T(8,128)(2,1)S(1)}, bf16[96,3584]{1,0:T(8,128)(2,1)S(1)}, u32[]{:S(2)}, u32[]{:S(2)}) collective-permute-start(bf16[96,3584]{1,0:T(8,128)(2,1)S(1)} %get-tuple-element.15), channel_id=1, source_target_pairs={{0,2},{1,3},{2,0},{3,1},{4,6},{5,7},{6,4},{7,5},{8,10},{9,11},{10,... | collective-permute-start | bytes 2064392 | tf_op jit(solution)/shard_map/ppermute | solution.py:25
  288.7 28.6 %collective-permute-start.26 = (bf16[96,3584]{1,0:T(8,128)(2,1)S(1)}, bf16[96,3584]{1,0:T(8,128)(2,1)S(1)}, u32[]{:S(2)}, u32[]{:S(2)}) collective-permute-start(bf16[96,3584]{1,0:T(8,128)(2,1)S(1)} %get-tuple-element.13), channel_id=1, source_target_pairs={{0,1},{1,0},{2,3},{3,2},{4,5},{5,4},{6,7},{7,6},{8,9},{9,8},{10,11... | collective-permute-start | bytes 2064392 | tf_op jit(solution)/shard_map/ppermute | solution.py:25
  320.2 30.9 %collective-permute-start.30 = (bf16[96,3584]{1,0:T(8,128)(2,1)S(1)}, bf16[96,3584]{1,0:T(8,128)(2,1)S(1)}, u32[]{:S(2)}, u32[]{:S(2)}) collective-permute-start(bf16[96,3584]{1,0:T(8,128)(2,1)S(1)} %multiply_convert_fusion), channel_id=1, source_target_pairs={{0,2},{1,3},{2,0},{3,1},{4,6},{5,7},{6,4},{7,5},{8,10},{9,11},{10,... | collective-permute-start | bytes 2064392 | tf_op jit(solution)/shard_map/ppermute | solution.py:25
  321.6 30.0 %collective-permute-start.29 = (bf16[96,3584]{1,0:T(8,128)(2,1)S(1)}, bf16[96,3584]{1,0:T(8,128)(2,1)S(1)}, u32[]{:S(2)}, u32[]{:S(2)}) collective-permute-start(bf16[96,3584]{1,0:T(8,128)(2,1)S(1)} %multiply_convert_fusion), channel_id=1, source_target_pairs={{0,1},{1,0},{2,3},{3,2},{4,5},{5,4},{6,7},{7,6},{8,9},{9,8},{10,11... | collective-permute-start | bytes 2064392 | tf_op jit(solution)/shard_map/ppermute | solution.py:25
  (19 other events, 398.5 us)
